TPU v7x, 32 devices: a whole 2x2x4 slice. The times are simulated.
32 devices in a mesh: space: 4 (over z), date: 8 (over y, x, core).
Axes of the slice: x: 2, y: 2, z: 4, core: 2. Of those that a mesh axis runs over, the one named last changes fastest.
Arguments:
- slc: bfloat16 [32, 128, 1024], P('date', 'space'), may hold values from -6 to 6
- footprint: int32 [128, 2], replicated, may hold values from -1 to 31, as said below
- valid_rows: int32 [4], P('space'), may hold values from 16 to 32
- pair_dates: int32 [528, 2], P('date'), may hold values from 0 to 31, as said below
Outputs:
- coherence: float32 [528, 4, 2, 8, 128], P('date', 'space')
Inputs may be any that keep to these rules, and one draw needn't show every extreme that they name: `footprint`: column 0 names a tile, or -1 for a block outside every tile; column 1 a row of that tile (0 for -1). No two blocks share a tile row. At most 8 blocks held by one index of space go to one tile, and for every tile exactly 8 come from some one index. `pair_dates`: each row names two dates, the first no later than the second; every one of the 528 pairs stands in some row.
All inputs are finite; a program needn't handle non-finite values.
Results may differ from a plain program's by a relative error of at most 0.0019.
Values may be sent and summed in bfloat16 or wider, within the bound.
A program may use at most 64 MiB of HBM per device.

v0:
```python
import functools

import jax
import jax.numpy as jnp
from jax import lax
from jax.experimental import pallas as pl
from jax.experimental.pallas import tpu as pltpu
from jax.sharding import PartitionSpec as P

CHUNKS = 4
Z_AHEAD = 2
MESH = pl.DeviceIdType.MESH
F32, BF16 = jnp.float32, jnp.bfloat16


def largest_divisor(count, most):
    return max(g for g in range(1, most + 1) if count % g == 0)


def partners(date, n_date):
    chips = n_date // 2
    chip, core = date // 2, date % 2
    sibling = chip * 2 + (1 - core)
    if chips == 4:
        x, y = chip % 2, chip // 2
        x1, y1 = core * x + (1 - core) * (1 - x), core * (1 - y) + (1 - core) * y
        x2, y2 = core * (1 - x) + (1 - core) * x, core * y + (1 - core) * (1 - y)
        others = [(y1 * 2 + x1) * 2 + core, (y2 * 2 + x2) * 2 + core, ((1 - y) * 2 + (1 - x)) * 2 + core]
        return sibling, others, others, True
    targets = [lax.rem(chip + k, chips) * 2 + core for k in range(1, chips)]
    sources = [lax.rem(chip + chips - k, chips) * 2 + core for k in range(1, chips)]
    return sibling, targets, sources, False


def tables(cfg, foot, valid, own):
    groups, n_date, dates_dev, blocks, width, cap, slots = cfg
    total, looks, lane = groups * blocks, blocks // 4, 128
    tile, row = foot[0:1], foot[1:2]

    def index(shape, dim):
        return lax.broadcasted_iota(jnp.int32, shape, dim)

    def ones(mask):
        return mask.astype(F32).astype(BF16)

    earlier = (index((lane, lane), 0) < index((lane, lane), 1)) & (
        lax.div(index((lane, lane), 0), blocks) == lax.div(index((lane, lane), 1), blocks)
    )
    ranks = []
    for at in range(0, total, lane):
        hot = index((max(groups, 8), lane), 0) == tile[:, at : at + lane]
        count = jnp.dot(ones(hot), ones(earlier), preferred_element_type=F32)
        ranks.append(jnp.sum(jnp.where(hot, count, 0.0), axis=0, keepdims=True))
    rank = jnp.concatenate(ranks, axis=1).astype(jnp.int32)

    n_slot, n_place = groups * dates_dev * cap, dates_dev * blocks
    slot = index((n_slot, total), 0)
    slot_group, slot_rank = lax.div(slot, dates_dev * cap), lax.rem(slot, cap)
    slot_date = lax.rem(lax.div(index((n_slot, n_place), 0), cap), dates_dev)
    fits = slot_rank == rank
    leaves = ones(fits & (slot_group == tile))
    held = ones(index((total, n_place), 0) == own * blocks + lax.rem(index((total, n_place), 1), blocks))
    select = jnp.dot(leaves, held, preferred_element_type=F32)
    select = jnp.where(slot_date == lax.div(index((n_slot, n_place), 1), blocks), select, 0.0)

    place_at = lax.rem(row, 4) * looks + lax.div(row, 4)
    place_at = jnp.where((tile == own) & (row < valid), place_at, -1)
    lands = ones(lax.rem(index((n_place, total), 0), blocks) == place_at)
    comes = ones(fits & (slot_group == lax.div(index((n_slot, total), 1), blocks)))
    place = lax.dot_general(lands, comes, (((1,), (1,)), ((), ())), preferred_element_type=F32)
    from_date = lax.rem(lax.div(index((n_place, n_slot), 1), cap), dates_dev)
    place = jnp.where(from_date == lax.div(index((n_place, n_slot), 0), blocks), place, 0.0)
    return select.astype(BF16), place.astype(BF16)


def kernel(cfg, slc_ref, foot_ref, valid_ref, pairs_ref, out_ref, *scratch):
    groups, n_date, dates_dev, blocks, width, cap, slots = cfg
    out_bufs, in_bufs = scratch[:CHUNKS], scratch[CHUNKS : 2 * CHUNKS]
    panels = scratch[2 * CHUNKS : 3 * CHUNKS]
    floor_ref, z_send, z_recv, d_send, d_recv, f_send, f_recv, c_send, c_recv = scratch[3 * CHUNKS :]
    wc = width // CHUNKS
    looks = blocks // 4
    dates = n_date * dates_dev
    own, date = lax.axis_index("space"), lax.axis_index("date")
    sibling, targets, sources, corner = partners(date, n_date)
    direct = targets[:2] if corner else targets
    peers = [lax.rem(own + k, groups) for k in range(1, groups)]

    barrier = pltpu.get_barrier_semaphore()
    for peer in peers:
        pl.semaphore_signal(barrier, inc=1, device_id={"space": peer}, device_id_type=MESH)
    for target in direct + [sibling]:
        pl.semaphore_signal(barrier, inc=1, device_id={"date": target}, device_id_type=MESH)

    select, place = tables(cfg, foot_ref[...], valid_ref[0], own)

    def gather_rows(c):
        for part in range(2):
            cols = slice(part * width + c * wc, part * width + (c + 1) * wc)
            rows = jnp.dot(select, slc_ref[:, cols], preferred_element_type=F32).astype(BF16)
            out_bufs[c][:, :, part * wc : (part + 1) * wc] = rows.reshape(groups, dates_dev * cap, wc)

    sends = []

    def z_copy(c, k):
        return pltpu.make_async_remote_copy(
            src_ref=out_bufs[c].at[peers[k]],
            dst_ref=in_bufs[c].at[own],
            send_sem=z_send.at[c, k],
            recv_sem=z_recv.at[c, k],
            device_id={"space": peers[k]},
            device_id_type=MESH,
        )

    def panel_copy(c, source, target, send_sem, recv_sem):
        block = panels[c].at[pl.ds(source * dates_dev, dates_dev)]
        return pltpu.make_async_remote_copy(
            src_ref=block,
            dst_ref=block,
            send_sem=send_sem,
            recv_sem=recv_sem,
            device_id={"date": target},
            device_id_type=MESH,
        )

    z_copies, d_copies, s_copies, r_copies = {}, {}, {}, {}

    def stage_send(c):
        gather_rows(c)
        if c == 0:
            pl.semaphore_wait(barrier, len(peers) + len(direct) + 1)
        for k in range(len(peers)):
            z_copies[c, k] = z_copy(c, k)
            if c < Z_AHEAD:
                z_copies[c, k].start()
        in_bufs[c][own] = out_bufs[c][own]

    def stage_place(c):
        for k in range(len(peers)):
            z_copies[c, k].wait_recv()
            if c + Z_AHEAD < CHUNKS:
                z_copies[c, k].wait_send()
                z_copies[c + Z_AHEAD, k].start()
        rows = in_bufs[c][...].reshape(groups * dates_dev * cap, 2 * wc)
        tile = jnp.dot(place, rows, preferred_element_type=F32).astype(BF16)
        panels[c][pl.ds(date * dates_dev, dates_dev)] = tile.reshape(dates_dev, blocks, 2 * wc)
        for k, target in enumerate(direct):
            d_copies[c, k] = panel_copy(c, date, target, d_send.at[c, k], d_recv.at[c, k])
            d_copies[c, k].start()
        s_copies[c] = panel_copy(c, date, sibling, c_send.at[c], c_recv.at[c])
        s_copies[c].start()

    def to_sibling(c, k):
        r_copies[c, k] = panel_copy(c, sources[k], sibling, f_send.at[c, k], f_recv.at[c, k])
        r_copies[c, k].start()

    def stage_forward(c):
        for k in range(len(direct)):
            if corner and k == 1:
                continue
            d_copies[c, k].wait_recv()
            if corner and k == 0:
                d_copies[c, 2] = panel_copy(c, sources[0], targets[1], d_send.at[c, 2], d_recv.at[c, 2])
                d_copies[c, 2].start()
            to_sibling(c, k)

    def stage_corner(c):
        if corner:
            d_copies[c, 1].wait_recv()
            to_sibling(c, 1)
            d_copies[c, 2].wait_recv()
            to_sibling(c, 2)

    def row_sum(summed, count):
        quads = summed.reshape(count, 4, looks, 128)
        last = lax.broadcasted_iota(jnp.int32, (count, looks, 128), 1) == looks - 1
        below = jnp.where(last, 0.0, pltpu.roll(quads[:, 0], looks - 1, 1))
        return quads[:, 0] + quads[:, 1] + quads[:, 2] + quads[:, 3] + below

    def stage_looks(c):
        s_copies[c].wait_recv()
        for k in range(len(sources)):
            r_copies[c, k].wait_recv()
        panel = panels[c]
        col_in = lax.broadcasted_iota(jnp.int32, (wc, 128), 0) + c * wc
        col_out = lax.broadcasted_iota(jnp.int32, (wc, 128), 1)
        table = (jnp.abs(col_in - 4 * col_out - 2) <= 5).astype(F32).astype(BF16)
        last = c == CHUNKS - 1

        group = largest_divisor(dates, max(1, 256 // blocks))

        def power_body(n, carry):
            rows = panel[pl.ds(n * group, group)].astype(F32)
            real, imag = rows[:, :, :wc], rows[:, :, wc:]
            power = (real * real + imag * imag).astype(BF16).reshape(group * blocks, wc)
            looked = row_sum(jnp.dot(power, table, preferred_element_type=F32), group)
            at = pl.ds(n * group, group)
            if c > 0:
                looked = looked + floor_ref[at]
            if last:
                looked = lax.rsqrt(jnp.maximum(looked, 1.0))
            floor_ref[at] = looked
            return carry

        lax.fori_loop(0, dates // group, power_body, 0, unroll=True)

        batch = largest_divisor(slots, max(1, 352 // blocks))

        def pair_body(n, carry):
            crosses, scales = [], []
            for g in range(batch):
                p = n * batch + g
                i, j = pairs_ref[0, p], pairs_ref[1, p]
                first, second = panel[i].astype(F32), panel[j].astype(F32)
                ra, ia, rb, ib = first[:, :wc], first[:, wc:], second[:, :wc], second[:, wc:]
                crosses.append((ra * rb + ia * ib).astype(BF16))
                crosses.append((ia * rb - ra * ib).astype(BF16))
                if last:
                    scales.append(floor_ref[i] * floor_ref[j])
            cross = jnp.concatenate(crosses, axis=0)
            looked = row_sum(jnp.dot(cross, table, preferred_element_type=F32), 2 * batch)
            looked = looked.reshape(batch, 2, looks, 128)
            at = pl.ds(n * batch, batch)
            if c > 0:
                looked = looked + out_ref[at]
            if last:
                looked = looked * jnp.stack(scales)[:, None]
            out_ref[at] = looked
            return carry

        lax.fori_loop(0, slots // batch, pair_body, 0, unroll=True)

    for step in range(CHUNKS):
        stage_send(step)
    for step in range(CHUNKS + 3):
        for lag, stage in enumerate((stage_place, stage_forward, stage_corner, stage_looks)):
            if 0 <= step - lag < CHUNKS:
                stage(step - lag)
    for copies in (z_copies, d_copies, s_copies, r_copies):
        for at, copy in copies.items():
            if copies is not z_copies or at[0] + Z_AHEAD >= CHUNKS:
                copy.wait_send()


def on_device(slc, footprint, valid_rows, pair_dates):
    groups, n_date = lax.axis_size("space"), lax.axis_size("date")
    dates_dev, blocks, twice = slc.shape
    width = twice // 2
    cap = blocks // groups
    slots = pair_dates.shape[0]
    looks = blocks // 4
    wc = width // CHUNKS
    others = n_date // 2 - 1
    sem = pltpu.SemaphoreType.DMA
    cfg = (groups, n_date, dates_dev, blocks, width, cap, slots)
    vmem, smem = pl.BlockSpec(memory_space=pltpu.VMEM), pl.BlockSpec(memory_space=pltpu.SMEM)
    result = pl.pallas_call(
        functools.partial(kernel, cfg),
        out_shape=jax.ShapeDtypeStruct((slots, 2, looks, 128), F32),
        in_specs=[vmem, vmem, smem, smem],
        out_specs=vmem,
        scratch_shapes=[pltpu.VMEM((groups, dates_dev * cap, 2 * wc), BF16)] * (2 * CHUNKS)
        + [pltpu.VMEM((n_date * dates_dev, blocks, 2 * wc), BF16)] * CHUNKS
        + [
            pltpu.VMEM((n_date * dates_dev, looks, 128), F32),
            sem((CHUNKS, groups - 1)),
            sem((CHUNKS, groups - 1)),
            sem((CHUNKS, others)),
            sem((CHUNKS, others)),
            sem((CHUNKS, others)),
            sem((CHUNKS, others)),
            sem((CHUNKS,)),
            sem((CHUNKS,)),
        ],
        compiler_params=pltpu.CompilerParams(
            collective_id=0, has_side_effects=True, vmem_limit_bytes=40 * 1024 * 1024
        ),
    )(slc.reshape(dates_dev * blocks, twice), footprint.T, valid_rows, pair_dates.T)
    return result[:, None]


def solution(mesh):
    in_specs = (P("date", "space", None), P(), P("space"), P("date", None))
    out_specs = P("date", "space", None, None, None)
    return jax.shard_map(
        on_device, mesh=mesh, in_specs=in_specs, out_specs=out_specs, check_vma=False
    )
```

profile of v0, /device:TPU:0, one launch (start us, length us, event | category | flops | bytes accessed | tf_op | source)
XLA Modules:
  0.0 27.7 jit_solution(4118988605848546880)
XLA Ops:
  0.7 0.0 copy-start.2
  0.7 0.0 copy-start.1
  0.7 0.7 %copy-done.2 = s32[66,2]{0,1:T(2,128)S(1)} copy-done((s32[66,2]{0,1:T(2,128)S(1)}, s32[66,2]{0,1:T(2,128)}, u32[]{:S(2)}) %copy-start.2) | copy-done | bytes 552
  1.3 0.0 copy-done.1
  1.3 0.0 copy-start
  1.4 0.9 %copy-done = bf16[4,32,1024]{2,1,0:T(8,128)(2,1)S(1)} copy-done((bf16[4,32,1024]{2,1,0:T(8,128)(2,1)S(1)}, bf16[4,32,1024]{2,1,0:T(8,128)(2,1)}, u32[]{:S(2)}) %copy-start) | copy-done | bytes 262168
  2.3 24.6 %shard_map.46 = f32[66,2,8,128]{3,2,1,0:T(8,128)S(1)} custom-call(bf16[128,1024]{1,0:T(8,128)(2,1)S(1)} %bitcast.7, s32[2,128]{1,0:T(2,128)S(1)} %bitcast.8, s32[1]{0:T(128)S(6)} %copy.7.valid_ref, s32[2,66]{1,0:T(2,128)S(1)} %bitcast.9), custom_call_target="tpu_custom_call" | custom-call | tf_op jit(solution)/shard_map/pallas_call | solution.py:257
  26.9 0.8 %copy.8 = f32[66,1,2,8,128]{4,3,2,1,0:T(8,128)} copy(f32[66,1,2,8,128]{4,3,2,1,0:T(8,128)S(1)} %bitcast.6) | data formatting | bytes 1081344
Async XLA Ops:
  0.7 0.7 %copy-start.2 = (s32[66,2]{0,1:T(2,128)S(1)}, s32[66,2]{0,1:T(2,128)}, u32[]{:S(2)}) copy-start(s32[66,2]{0,1:T(2,128)} %param.7) | copy-start | bytes 1588
  0.7 0.7 %copy-start.1 = (s32[128,2]{0,1:T(2,128)S(1)}, s32[128,2]{0,1:T(2,128)}, u32[]{:S(2)}) copy-start(s32[128,2]{0,1:T(2,128)} %param.5) | copy-start | bytes 3076
  1.3 0.9 %copy-start = (bf16[4,32,1024]{2,1,0:T(8,128)(2,1)S(1)}, bf16[4,32,1024]{2,1,0:T(8,128)(2,1)}, u32[]{:S(2)}) copy-start(bf16[4,32,1024]{2,1,0:T(8,128)(2,1)} %param.4) | copy-start | bytes 786436
where the time goes:
time: 27.9 us; the launch traced here: 27.7 us
  Pallas kernels  24.6 us (88%)
  local copies, waits for them, and re-layouts  2.43 us (9%)
  between operations  0.68 us (2%)
    pallas_call x1, Pallas kernels, on_device(): pl.pallas_call(functools.partial(kernel, cfg), out_shape=jax.ShapeDtypeSt...  24.6 us
    unnamed x7, local copies, waits for them, and re-layouts  2.43 us

commit v1 on v0

--- a/solution.py
+++ b/solution.py
@@ -73,11 +73,13 @@
     return select.astype(BF16), place.astype(BF16)
 
 
-def kernel(cfg, slc_ref, foot_ref, valid_ref, pairs_ref, out_ref, *scratch):
+def kernel(cfg, slc_hbm, foot_hbm, valid_ref, pairs_hbm, out_ref, *scratch):
     groups, n_date, dates_dev, blocks, width, cap, slots = cfg
     out_bufs, in_bufs = scratch[:CHUNKS], scratch[CHUNKS : 2 * CHUNKS]
     panels = scratch[2 * CHUNKS : 3 * CHUNKS]
-    floor_ref, z_send, z_recv, d_send, d_recv, f_send, f_recv, c_send, c_recv = scratch[3 * CHUNKS :]
+    rest = scratch[3 * CHUNKS :]
+    floor_ref, z_send, z_recv, d_send, d_recv, f_send, f_recv, c_send, c_recv = rest[:9]
+    slc_ref, foot_ref, pairs_ref, in_sem = rest[9:]
     wc = width // CHUNKS
     looks = blocks // 4
     dates = n_date * dates_dev
@@ -92,7 +94,16 @@
     for target in direct + [sibling]:
         pl.semaphore_signal(barrier, inc=1, device_id={"date": target}, device_id_type=MESH)
 
+    fetches = [
+        pltpu.make_async_copy(src, dst, in_sem.at[k])
+        for k, (src, dst) in enumerate([(foot_hbm, foot_ref), (slc_hbm, slc_ref), (pairs_hbm, pairs_ref)])
+    ]
+    for fetch in fetches:
+        fetch.start()
+    fetches[0].wait()
     select, place = tables(cfg, foot_ref[...], valid_ref[0], own)
+    fetches[1].wait()
+    fetches[2].wait()
 
     def gather_rows(c):
         for part in range(2):
@@ -253,12 +264,13 @@
     others = n_date // 2 - 1
     sem = pltpu.SemaphoreType.DMA
     cfg = (groups, n_date, dates_dev, blocks, width, cap, slots)
-    vmem, smem = pl.BlockSpec(memory_space=pltpu.VMEM), pl.BlockSpec(memory_space=pltpu.SMEM)
+    far = functools.partial(pltpu.with_memory_space_constraint, memory_space=pltpu.HBM)
+    hbm, smem = pl.BlockSpec(memory_space=pltpu.HBM), pl.BlockSpec(memory_space=pltpu.SMEM)
     result = pl.pallas_call(
         functools.partial(kernel, cfg),
         out_shape=jax.ShapeDtypeStruct((slots, 2, looks, 128), F32),
-        in_specs=[vmem, vmem, smem, smem],
-        out_specs=vmem,
+        in_specs=[hbm, hbm, smem, hbm],
+        out_specs=pl.BlockSpec(memory_space=pltpu.VMEM),
         scratch_shapes=[pltpu.VMEM((groups, dates_dev * cap, 2 * wc), BF16)] * (2 * CHUNKS)
         + [pltpu.VMEM((n_date * dates_dev, blocks, 2 * wc), BF16)] * CHUNKS
         + [
@@ -271,11 +283,15 @@
             sem((CHUNKS, others)),
             sem((CHUNKS,)),
             sem((CHUNKS,)),
+            pltpu.VMEM((dates_dev * blocks, twice), BF16),
+            pltpu.VMEM(footprint.shape[::-1], jnp.int32),
+            pltpu.SMEM(pair_dates.shape[::-1], jnp.int32),
+            sem((3,)),
         ],
         compiler_params=pltpu.CompilerParams(
             collective_id=0, has_side_effects=True, vmem_limit_bytes=40 * 1024 * 1024
         ),
-    )(slc.reshape(dates_dev * blocks, twice), footprint.T, valid_rows, pair_dates.T)
+    )(far(slc.reshape(dates_dev * blocks, twice)), far(footprint.T), valid_rows, far(pair_dates.T))
     return result[:, None]
 
 

time: 27.9 us -> 25.7 us (0.921)
  local copies, waits for them, and re-layouts: 2.43 us -> 0.8 us
  Pallas kernels: 24.6 us -> 24.1 us
    unnamed x7 -> x1, local copies, waits for them, and re-layouts: 2.43 us -> 0.8 us
    pallas_call x1, Pallas kernels: 24.6 us -> 24.1 us  [on_device(): pl.pallas_call(functools.partial(kernel, cfg), out_shape=jax.ShapeDtypeSt...]
where the time goes in v1:
time: 25.7 us; the launch traced here: 25.5 us
  Pallas kernels  24.1 us (94%)
  local copies, waits for them, and re-layouts  0.8 us (3%)
  between operations  0.66 us (3%)
    pallas_call x1, Pallas kernels, on_device(): pl.pallas_call(functools.partial(kernel, cfg), out_shape=jax.ShapeDtypeSt...  24.1 us
    unnamed x1, local copies, waits for them, and re-layouts  0.8 us

profile of v1, /device:TPU:0, one launch (start us, length us, event | category | flops | bytes accessed | tf_op | source)
XLA Modules:
  0.0 25.5 jit_solution(1171245018172735894)
XLA Ops:
  0.7 24.1 %shard_map.46 = f32[66,2,8,128]{3,2,1,0:T(8,128)S(1)} custom-call(bf16[128,1024]{1,0:T(8,128)(2,1)} %bitcast.7, s32[2,128]{1,0:T(2,128)} %bitcast.8, s32[1]{0:T(128)S(6)} %copy.7.valid_ref, s32[2,66]{1,0:T(2,128)} %bitcast.9), custom_call_target="tpu_custom_call" | custom-call | tf_op jit(solution)/shard_map/pallas_call | solution.py:269
  24.7 0.8 %copy.8 = f32[66,1,2,8,128]{4,3,2,1,0:T(8,128)} copy(f32[66,1,2,8,128]{4,3,2,1,0:T(8,128)S(1)} %bitcast.6) | data formatting | bytes 1081344

commit v2 on v1

--- a/solution.py
+++ b/solution.py
@@ -7,8 +7,10 @@
 from jax.experimental.pallas import tpu as pltpu
 from jax.sharding import PartitionSpec as P
 
-CHUNKS = 4
-Z_AHEAD = 2
+WIDTHS = (1, 2, 1)
+CHUNKS = len(WIDTHS)
+RELAYED = ((False, False, False), (False, False, False))
+ORDER = (('z', 0), ('z', 1), ('z', 2), ('e', 0), ('e', 1), ('e', 2), ('o', 0), ('o', 1), ('o', 2), ('f', 0), ('f', 1), ('c', 0), ('c', 1), ('l', 0), ('f', 2), ('c', 2), ('l', 1), ('l', 2))
 MESH = pl.DeviceIdType.MESH
 F32, BF16 = jnp.float32, jnp.bfloat16
 
@@ -36,6 +38,7 @@
     groups, n_date, dates_dev, blocks, width, cap, slots = cfg
     total, looks, lane = groups * blocks, blocks // 4, 128
     tile, row = foot[0:1], foot[1:2]
+    tile_step = jnp.where(tile < 0, -1, lax.rem(tile - own + groups, groups))
 
     def index(shape, dim):
         return lax.broadcasted_iota(jnp.int32, shape, dim)
@@ -58,7 +61,7 @@
     slot_group, slot_rank = lax.div(slot, dates_dev * cap), lax.rem(slot, cap)
     slot_date = lax.rem(lax.div(index((n_slot, n_place), 0), cap), dates_dev)
     fits = slot_rank == rank
-    leaves = ones(fits & (slot_group == tile))
+    leaves = ones(fits & (slot_group == tile_step))
     held = ones(index((total, n_place), 0) == own * blocks + lax.rem(index((total, n_place), 1), blocks))
     select = jnp.dot(leaves, held, preferred_element_type=F32)
     select = jnp.where(slot_date == lax.div(index((n_slot, n_place), 1), blocks), select, 0.0)
@@ -66,7 +69,8 @@
     place_at = lax.rem(row, 4) * looks + lax.div(row, 4)
     place_at = jnp.where((tile == own) & (row < valid), place_at, -1)
     lands = ones(lax.rem(index((n_place, total), 0), blocks) == place_at)
-    comes = ones(fits & (slot_group == lax.div(index((n_slot, total), 1), blocks)))
+    from_step = lax.rem(lax.div(index((n_slot, total), 1), blocks) - own + groups, groups)
+    comes = ones(fits & (slot_group == from_step))
     place = lax.dot_general(lands, comes, (((1,), (1,)), ((), ())), preferred_element_type=F32)
     from_date = lax.rem(lax.div(index((n_place, n_slot), 1), cap), dates_dev)
     place = jnp.where(from_date == lax.div(index((n_place, n_slot), 0), blocks), place, 0.0)
@@ -75,23 +79,24 @@
 
 def kernel(cfg, slc_hbm, foot_hbm, valid_ref, pairs_hbm, out_ref, *scratch):
     groups, n_date, dates_dev, blocks, width, cap, slots = cfg
-    out_bufs, in_bufs = scratch[:CHUNKS], scratch[CHUNKS : 2 * CHUNKS]
+    out_bufs, slot_bufs = scratch[:CHUNKS], scratch[CHUNKS : 2 * CHUNKS]
     panels = scratch[2 * CHUNKS : 3 * CHUNKS]
     rest = scratch[3 * CHUNKS :]
     floor_ref, z_send, z_recv, d_send, d_recv, f_send, f_recv, c_send, c_recv = rest[:9]
     slc_ref, foot_ref, pairs_ref, in_sem = rest[9:]
-    wc = width // CHUNKS
     looks = blocks // 4
     dates = n_date * dates_dev
     own, date = lax.axis_index("space"), lax.axis_index("date")
     sibling, targets, sources, corner = partners(date, n_date)
-    direct = targets[:2] if corner else targets
     peers = [lax.rem(own + k, groups) for k in range(1, groups)]
+
+    wide = [width * w // sum(WIDTHS) for w in WIDTHS]
+    left = [sum(wide[:c]) for c in range(CHUNKS)]
 
     barrier = pltpu.get_barrier_semaphore()
     for peer in peers:
         pl.semaphore_signal(barrier, inc=1, device_id={"space": peer}, device_id_type=MESH)
-    for target in direct + [sibling]:
+    for target in targets + [sibling]:
         pl.semaphore_signal(barrier, inc=1, device_id={"date": target}, device_id_type=MESH)
 
     fetches = [
@@ -106,25 +111,28 @@
     fetches[2].wait()
 
     def gather_rows(c):
+        wc = wide[c]
         for part in range(2):
-            cols = slice(part * width + c * wc, part * width + (c + 1) * wc)
+            cols = slice(part * width + left[c], part * width + left[c] + wc)
+            half = slice(part * wc, (part + 1) * wc)
             rows = jnp.dot(select, slc_ref[:, cols], preferred_element_type=F32).astype(BF16)
-            out_bufs[c][:, :, part * wc : (part + 1) * wc] = rows.reshape(groups, dates_dev * cap, wc)
-
-    sends = []
+            rows = rows.reshape(groups, dates_dev * cap, wc)
+            slot_bufs[c][date, 0, :, half] = rows[0]
+            out_bufs[c][:, :, half] = rows[1:]
 
     def z_copy(c, k):
         return pltpu.make_async_remote_copy(
-            src_ref=out_bufs[c].at[peers[k]],
-            dst_ref=in_bufs[c].at[own],
+            src_ref=out_bufs[c].at[k],
+            dst_ref=slot_bufs[c].at[date, groups - 1 - k],
             send_sem=z_send.at[c, k],
             recv_sem=z_recv.at[c, k],
             device_id={"space": peers[k]},
             device_id_type=MESH,
         )
 
-    def panel_copy(c, source, target, send_sem, recv_sem):
-        block = panels[c].at[pl.ds(source * dates_dev, dates_dev)]
+    def slot_copy(c, part, source, target, send_sem, recv_sem):
+        steps = pl.ds(0, 1) if part == 0 else pl.ds(1, groups - 1)
+        block = slot_bufs[c].at[source, steps]
         return pltpu.make_async_remote_copy(
             src_ref=block,
             dst_ref=block,
@@ -136,50 +144,74 @@
 
     z_copies, d_copies, s_copies, r_copies = {}, {}, {}, {}
 
+    def relayed(c, part):
+        return corner and RELAYED[part][c]
+
+    def send(c, part):
+        for k, target in enumerate(targets[:2] if relayed(c, part) else targets):
+            d_copies[c, part, k] = slot_copy(c, part, date, target, d_send.at[c, part, k], d_recv.at[c, part, k])
+            d_copies[c, part, k].start()
+
+    def panel_copy(c, source, send_sem, recv_sem):
+        block = panels[c].at[pl.ds(source * dates_dev, dates_dev)]
+        return pltpu.make_async_remote_copy(
+            src_ref=block,
+            dst_ref=block,
+            send_sem=send_sem,
+            recv_sem=recv_sem,
+            device_id={"date": sibling},
+            device_id_type=MESH,
+        )
+
+    def fill(c, source):
+        wc = wide[c]
+        rows = slot_bufs[c][source].reshape(groups * dates_dev * cap, 2 * wc)
+        tile = jnp.dot(place, rows, preferred_element_type=F32).astype(BF16)
+        panels[c][pl.ds(source * dates_dev, dates_dev)] = tile.reshape(dates_dev, blocks, 2 * wc)
+
+    def arrive(c, part, k):
+        d_copies[c, part, k].wait_recv()
+        if k == 0 and relayed(c, part):
+            relay = slot_copy(c, part, sources[0], targets[1], d_send.at[c, part, 2], d_recv.at[c, part, 2])
+            d_copies[c, part, 2] = relay
+            relay.start()
+
+    def to_sibling(c, k):
+        arrive(c, 1, k)
+        fill(c, sources[k])
+        r_copies[c, k] = panel_copy(c, sources[k], f_send.at[c, k], f_recv.at[c, k])
+        r_copies[c, k].start()
+
     def stage_send(c):
         gather_rows(c)
         if c == 0:
-            pl.semaphore_wait(barrier, len(peers) + len(direct) + 1)
+            pl.semaphore_wait(barrier, len(peers) + len(targets) + 1)
         for k in range(len(peers)):
             z_copies[c, k] = z_copy(c, k)
-            if c < Z_AHEAD:
-                z_copies[c, k].start()
-        in_bufs[c][own] = out_bufs[c][own]
-
-    def stage_place(c):
+            z_copies[c, k].start()
+        send(c, 0)
+
+    def stage_z(c):
         for k in range(len(peers)):
             z_copies[c, k].wait_recv()
-            if c + Z_AHEAD < CHUNKS:
-                z_copies[c, k].wait_send()
-                z_copies[c + Z_AHEAD, k].start()
-        rows = in_bufs[c][...].reshape(groups * dates_dev * cap, 2 * wc)
-        tile = jnp.dot(place, rows, preferred_element_type=F32).astype(BF16)
-        panels[c][pl.ds(date * dates_dev, dates_dev)] = tile.reshape(dates_dev, blocks, 2 * wc)
-        for k, target in enumerate(direct):
-            d_copies[c, k] = panel_copy(c, date, target, d_send.at[c, k], d_recv.at[c, k])
-            d_copies[c, k].start()
-        s_copies[c] = panel_copy(c, date, sibling, c_send.at[c], c_recv.at[c])
+        send(c, 1)
+
+    def stage_own(c):
+        fill(c, date)
+        s_copies[c] = panel_copy(c, date, c_send.at[c], c_recv.at[c])
         s_copies[c].start()
 
-    def to_sibling(c, k):
-        r_copies[c, k] = panel_copy(c, sources[k], sibling, f_send.at[c, k], f_recv.at[c, k])
-        r_copies[c, k].start()
+    def stage_early(c):
+        for k in range(len(sources)):
+            arrive(c, 0, k)
 
     def stage_forward(c):
-        for k in range(len(direct)):
-            if corner and k == 1:
-                continue
-            d_copies[c, k].wait_recv()
-            if corner and k == 0:
-                d_copies[c, 2] = panel_copy(c, sources[0], targets[1], d_send.at[c, 2], d_recv.at[c, 2])
-                d_copies[c, 2].start()
+        for k in range(1 if relayed(c, 1) else len(sources)):
             to_sibling(c, k)
 
     def stage_corner(c):
-        if corner:
-            d_copies[c, 1].wait_recv()
+        if relayed(c, 1):
             to_sibling(c, 1)
-            d_copies[c, 2].wait_recv()
             to_sibling(c, 2)
 
     def row_sum(summed, count):
@@ -192,8 +224,8 @@
         s_copies[c].wait_recv()
         for k in range(len(sources)):
             r_copies[c, k].wait_recv()
-        panel = panels[c]
-        col_in = lax.broadcasted_iota(jnp.int32, (wc, 128), 0) + c * wc
+        panel, wc = panels[c], wide[c]
+        col_in = lax.broadcasted_iota(jnp.int32, (wc, 128), 0) + left[c]
         col_out = lax.broadcasted_iota(jnp.int32, (wc, 128), 1)
         table = (jnp.abs(col_in - 4 * col_out - 2) <= 5).astype(F32).astype(BF16)
         last = c == CHUNKS - 1
@@ -241,16 +273,21 @@
 
         lax.fori_loop(0, slots // batch, pair_body, 0, unroll=True)
 
-    for step in range(CHUNKS):
-        stage_send(step)
-    for step in range(CHUNKS + 3):
-        for lag, stage in enumerate((stage_place, stage_forward, stage_corner, stage_looks)):
-            if 0 <= step - lag < CHUNKS:
-                stage(step - lag)
+    for c in range(CHUNKS):
+        stage_send(c)
+    stages = {
+        "z": stage_z,
+        "o": stage_own,
+        "e": stage_early,
+        "f": stage_forward,
+        "c": stage_corner,
+        "l": stage_looks,
+    }
+    for name, c in ORDER:
+        stages[name](c)
     for copies in (z_copies, d_copies, s_copies, r_copies):
-        for at, copy in copies.items():
-            if copies is not z_copies or at[0] + Z_AHEAD >= CHUNKS:
-                copy.wait_send()
+        for copy in copies.values():
+            copy.wait_send()
 
 
 def on_device(slc, footprint, valid_rows, pair_dates):
@@ -260,7 +297,7 @@
     cap = blocks // groups
     slots = pair_dates.shape[0]
     looks = blocks // 4
-    wc = width // CHUNKS
+    wide = [width * w // sum(WIDTHS) for w in WIDTHS]
     others = n_date // 2 - 1
     sem = pltpu.SemaphoreType.DMA
     cfg = (groups, n_date, dates_dev, blocks, width, cap, slots)
@@ -271,14 +308,15 @@
         out_shape=jax.ShapeDtypeStruct((slots, 2, looks, 128), F32),
         in_specs=[hbm, hbm, smem, hbm],
         out_specs=pl.BlockSpec(memory_space=pltpu.VMEM),
-        scratch_shapes=[pltpu.VMEM((groups, dates_dev * cap, 2 * wc), BF16)] * (2 * CHUNKS)
-        + [pltpu.VMEM((n_date * dates_dev, blocks, 2 * wc), BF16)] * CHUNKS
+        scratch_shapes=[pltpu.VMEM((groups - 1, dates_dev * cap, 2 * wc), BF16) for wc in wide]
+        + [pltpu.VMEM((n_date, groups, dates_dev * cap, 2 * wc), BF16) for wc in wide]
+        + [pltpu.VMEM((n_date * dates_dev, blocks, 2 * wc), BF16) for wc in wide]
         + [
             pltpu.VMEM((n_date * dates_dev, looks, 128), F32),
             sem((CHUNKS, groups - 1)),
             sem((CHUNKS, groups - 1)),
-            sem((CHUNKS, others)),
-            sem((CHUNKS, others)),
+            sem((CHUNKS, 2, others)),
+            sem((CHUNKS, 2, others)),
             sem((CHUNKS, others)),
             sem((CHUNKS, others)),
             sem((CHUNKS,)),

time: 25.7 us -> 24.3 us (0.946)
  Pallas kernels: 24.1 us -> 22.7 us
    pallas_call x1, Pallas kernels: 24.1 us -> 22.7 us  [on_device(): pl.pallas_call(functools.partial(kernel, cfg), out_shape=jax.ShapeDtypeSt...]
where the time goes in v2:
time: 24.3 us; the launch traced here: 24.2 us
  Pallas kernels  22.7 us (93%)
  local copies, waits for them, and re-layouts  0.8 us (3%)
  between operations  0.66 us (3%)
    pallas_call x1, Pallas kernels, on_device(): pl.pallas_call(functools.partial(kernel, cfg), out_shape=jax.ShapeDtypeSt...  22.7 us
    unnamed x1, local copies, waits for them, and re-layouts  0.8 us

profile of v2, /device:TPU:0, one launch (start us, length us, event | category | flops | bytes accessed | tf_op | source)
XLA Modules:
  0.0 24.2 jit_solution(3824144099712603621)
XLA Ops:
  0.7 22.7 %shard_map.46 = f32[66,2,8,128]{3,2,1,0:T(8,128)S(1)} custom-call(bf16[128,1024]{1,0:T(8,128)(2,1)} %bitcast.7, s32[2,128]{1,0:T(2,128)} %bitcast.8, s32[1]{0:T(128)S(6)} %copy.7.valid_ref, s32[2,66]{1,0:T(2,128)} %bitcast.9), custom_call_target="tpu_custom_call" | custom-call | tf_op jit(solution)/shard_map/pallas_call | solution.py:306
  23.4 0.8 %copy.8 = f32[66,1,2,8,128]{4,3,2,1,0:T(8,128)} copy(f32[66,1,2,8,128]{4,3,2,1,0:T(8,128)S(1)} %bitcast.6) | data formatting | bytes 1081344

commit v3 on v2

--- a/solution.py
+++ b/solution.py
@@ -7,10 +7,8 @@
 from jax.experimental.pallas import tpu as pltpu
 from jax.sharding import PartitionSpec as P
 
-WIDTHS = (1, 2, 1)
-CHUNKS = len(WIDTHS)
-RELAYED = ((False, False, False), (False, False, False))
-ORDER = (('z', 0), ('z', 1), ('z', 2), ('e', 0), ('e', 1), ('e', 2), ('o', 0), ('o', 1), ('o', 2), ('f', 0), ('f', 1), ('c', 0), ('c', 1), ('l', 0), ('f', 2), ('c', 2), ('l', 1), ('l', 2))
+CHUNKS = 4
+BATCH_ROWS, GROUP_ROWS = 1056, 1024
 MESH = pl.DeviceIdType.MESH
 F32, BF16 = jnp.float32, jnp.bfloat16
 
@@ -23,15 +21,9 @@
     chips = n_date // 2
     chip, core = date // 2, date % 2
     sibling = chip * 2 + (1 - core)
-    if chips == 4:
-        x, y = chip % 2, chip // 2
-        x1, y1 = core * x + (1 - core) * (1 - x), core * (1 - y) + (1 - core) * y
-        x2, y2 = core * (1 - x) + (1 - core) * x, core * y + (1 - core) * (1 - y)
-        others = [(y1 * 2 + x1) * 2 + core, (y2 * 2 + x2) * 2 + core, ((1 - y) * 2 + (1 - x)) * 2 + core]
-        return sibling, others, others, True
     targets = [lax.rem(chip + k, chips) * 2 + core for k in range(1, chips)]
     sources = [lax.rem(chip + chips - k, chips) * 2 + core for k in range(1, chips)]
-    return sibling, targets, sources, False
+    return sibling, targets, sources
 
 
 def tables(cfg, foot, valid, own):
@@ -84,14 +76,12 @@
     rest = scratch[3 * CHUNKS :]
     floor_ref, z_send, z_recv, d_send, d_recv, f_send, f_recv, c_send, c_recv = rest[:9]
     slc_ref, foot_ref, pairs_ref, in_sem = rest[9:]
+    wc = width // CHUNKS
     looks = blocks // 4
     dates = n_date * dates_dev
     own, date = lax.axis_index("space"), lax.axis_index("date")
-    sibling, targets, sources, corner = partners(date, n_date)
+    sibling, targets, sources = partners(date, n_date)
     peers = [lax.rem(own + k, groups) for k in range(1, groups)]
-
-    wide = [width * w // sum(WIDTHS) for w in WIDTHS]
-    left = [sum(wide[:c]) for c in range(CHUNKS)]
 
     barrier = pltpu.get_barrier_semaphore()
     for peer in peers:
@@ -111,9 +101,8 @@
     fetches[2].wait()
 
     def gather_rows(c):
-        wc = wide[c]
         for part in range(2):
-            cols = slice(part * width + left[c], part * width + left[c] + wc)
+            cols = slice(part * width + c * wc, part * width + c * wc + wc)
             half = slice(part * wc, (part + 1) * wc)
             rows = jnp.dot(select, slc_ref[:, cols], preferred_element_type=F32).astype(BF16)
             rows = rows.reshape(groups, dates_dev * cap, wc)
@@ -130,9 +119,9 @@
             device_id_type=MESH,
         )
 
-    def slot_copy(c, part, source, target, send_sem, recv_sem):
+    def slot_copy(c, part, target, send_sem, recv_sem):
         steps = pl.ds(0, 1) if part == 0 else pl.ds(1, groups - 1)
-        block = slot_bufs[c].at[source, steps]
+        block = slot_bufs[c].at[date, steps]
         return pltpu.make_async_remote_copy(
             src_ref=block,
             dst_ref=block,
@@ -144,12 +133,9 @@
 
     z_copies, d_copies, s_copies, r_copies = {}, {}, {}, {}
 
-    def relayed(c, part):
-        return corner and RELAYED[part][c]
-
     def send(c, part):
-        for k, target in enumerate(targets[:2] if relayed(c, part) else targets):
-            d_copies[c, part, k] = slot_copy(c, part, date, target, d_send.at[c, part, k], d_recv.at[c, part, k])
+        for k, target in enumerate(targets):
+            d_copies[c, part, k] = slot_copy(c, part, target, d_send.at[c, part, k], d_recv.at[c, part, k])
             d_copies[c, part, k].start()
 
     def panel_copy(c, source, send_sem, recv_sem):
@@ -164,20 +150,13 @@
         )
 
     def fill(c, source):
-        wc = wide[c]
         rows = slot_bufs[c][source].reshape(groups * dates_dev * cap, 2 * wc)
         tile = jnp.dot(place, rows, preferred_element_type=F32).astype(BF16)
         panels[c][pl.ds(source * dates_dev, dates_dev)] = tile.reshape(dates_dev, blocks, 2 * wc)
 
-    def arrive(c, part, k):
-        d_copies[c, part, k].wait_recv()
-        if k == 0 and relayed(c, part):
-            relay = slot_copy(c, part, sources[0], targets[1], d_send.at[c, part, 2], d_recv.at[c, part, 2])
-            d_copies[c, part, 2] = relay
-            relay.start()
-
     def to_sibling(c, k):
-        arrive(c, 1, k)
+        for part in range(2):
+            d_copies[c, part, k].wait_recv()
         fill(c, sources[k])
         r_copies[c, k] = panel_copy(c, sources[k], f_send.at[c, k], f_recv.at[c, k])
         r_copies[c, k].start()
@@ -201,42 +180,38 @@
         s_copies[c] = panel_copy(c, date, c_send.at[c], c_recv.at[c])
         s_copies[c].start()
 
-    def stage_early(c):
+    def stage_forward(c):
         for k in range(len(sources)):
-            arrive(c, 0, k)
-
-    def stage_forward(c):
-        for k in range(1 if relayed(c, 1) else len(sources)):
             to_sibling(c, k)
 
-    def stage_corner(c):
-        if relayed(c, 1):
-            to_sibling(c, 1)
-            to_sibling(c, 2)
-
-    def row_sum(summed, count):
-        quads = summed.reshape(count, 4, looks, 128)
-        last = lax.broadcasted_iota(jnp.int32, (count, looks, 128), 1) == looks - 1
-        below = jnp.where(last, 0.0, pltpu.roll(quads[:, 0], looks - 1, 1))
-        return quads[:, 0] + quads[:, 1] + quads[:, 2] + quads[:, 3] + below
+    def row_sum(field):
+        quads = field.reshape(4, looks, field.shape[1])
+        last = lax.broadcasted_iota(jnp.int32, quads[0].shape, 0) == looks - 1
+        below = jnp.where(last, 0.0, pltpu.roll(quads[0], looks - 1, 0))
+        return (quads[0] + quads[1]) + (quads[2] + quads[3]) + below
+
+    def col_sum(rows, table):
+        return jnp.dot(rows.astype(BF16), table, preferred_element_type=F32)
 
     def stage_looks(c):
         s_copies[c].wait_recv()
         for k in range(len(sources)):
             r_copies[c, k].wait_recv()
-        panel, wc = panels[c], wide[c]
-        col_in = lax.broadcasted_iota(jnp.int32, (wc, 128), 0) + left[c]
+        panel = panels[c]
+        col_in = lax.broadcasted_iota(jnp.int32, (wc, 128), 0) + c * wc
         col_out = lax.broadcasted_iota(jnp.int32, (wc, 128), 1)
         table = (jnp.abs(col_in - 4 * col_out - 2) <= 5).astype(F32).astype(BF16)
         last = c == CHUNKS - 1
 
-        group = largest_divisor(dates, max(1, 256 // blocks))
+        group = largest_divisor(dates, max(1, GROUP_ROWS // blocks))
 
         def power_body(n, carry):
-            rows = panel[pl.ds(n * group, group)].astype(F32)
-            real, imag = rows[:, :, :wc], rows[:, :, wc:]
-            power = (real * real + imag * imag).astype(BF16).reshape(group * blocks, wc)
-            looked = row_sum(jnp.dot(power, table, preferred_element_type=F32), group)
+            sums = []
+            for g in range(group):
+                rows = panel[n * group + g].astype(F32)
+                real, imag = rows[:, :wc], rows[:, wc:]
+                sums.append(row_sum(real * real + imag * imag))
+            looked = col_sum(jnp.concatenate(sums, axis=0), table).reshape(group, looks, 128)
             at = pl.ds(n * group, group)
             if c > 0:
                 looked = looked + floor_ref[at]
@@ -247,22 +222,20 @@
 
         lax.fori_loop(0, dates // group, power_body, 0, unroll=True)
 
-        batch = largest_divisor(slots, max(1, 352 // blocks))
+        batch = largest_divisor(slots, max(1, BATCH_ROWS // blocks))
 
         def pair_body(n, carry):
-            crosses, scales = [], []
+            sums, scales = [], []
             for g in range(batch):
                 p = n * batch + g
                 i, j = pairs_ref[0, p], pairs_ref[1, p]
                 first, second = panel[i].astype(F32), panel[j].astype(F32)
                 ra, ia, rb, ib = first[:, :wc], first[:, wc:], second[:, :wc], second[:, wc:]
-                crosses.append((ra * rb + ia * ib).astype(BF16))
-                crosses.append((ia * rb - ra * ib).astype(BF16))
+                sums.append(row_sum(ra * rb + ia * ib))
+                sums.append(row_sum(ia * rb - ra * ib))
                 if last:
                     scales.append(floor_ref[i] * floor_ref[j])
-            cross = jnp.concatenate(crosses, axis=0)
-            looked = row_sum(jnp.dot(cross, table, preferred_element_type=F32), 2 * batch)
-            looked = looked.reshape(batch, 2, looks, 128)
+            looked = col_sum(jnp.concatenate(sums, axis=0), table).reshape(batch, 2, looks, 128)
             at = pl.ds(n * batch, batch)
             if c > 0:
                 looked = looked + out_ref[at]
@@ -275,16 +248,16 @@
 
     for c in range(CHUNKS):
         stage_send(c)
-    stages = {
-        "z": stage_z,
-        "o": stage_own,
-        "e": stage_early,
-        "f": stage_forward,
-        "c": stage_corner,
-        "l": stage_looks,
-    }
-    for name, c in ORDER:
-        stages[name](c)
+    for c in range(CHUNKS):
+        stage_z(c)
+    for c in range(CHUNKS):
+        stage_own(c)
+    for c in range(CHUNKS):
+        stage_forward(c)
+        if c > 1:
+            stage_looks(c - 2)
+    for c in range(max(CHUNKS - 2, 0), CHUNKS):
+        stage_looks(c)
     for copies in (z_copies, d_copies, s_copies, r_copies):
         for copy in copies.values():
             copy.wait_send()
@@ -297,7 +270,7 @@
     cap = blocks // groups
     slots = pair_dates.shape[0]
     looks = blocks // 4
-    wide = [width * w // sum(WIDTHS) for w in WIDTHS]
+    wc = width // CHUNKS
     others = n_date // 2 - 1
     sem = pltpu.SemaphoreType.DMA
     cfg = (groups, n_date, dates_dev, blocks, width, cap, slots)
@@ -308,9 +281,9 @@
         out_shape=jax.ShapeDtypeStruct((slots, 2, looks, 128), F32),
         in_specs=[hbm, hbm, smem, hbm],
         out_specs=pl.BlockSpec(memory_space=pltpu.VMEM),
-        scratch_shapes=[pltpu.VMEM((groups - 1, dates_dev * cap, 2 * wc), BF16) for wc in wide]
-        + [pltpu.VMEM((n_date, groups, dates_dev * cap, 2 * wc), BF16) for wc in wide]
-        + [pltpu.VMEM((n_date * dates_dev, blocks, 2 * wc), BF16) for wc in wide]
+        scratch_shapes=[pltpu.VMEM((groups - 1, dates_dev * cap, 2 * wc), BF16)] * CHUNKS
+        + [pltpu.VMEM((n_date, groups, dates_dev * cap, 2 * wc), BF16)] * CHUNKS
+        + [pltpu.VMEM((n_date * dates_dev, blocks, 2 * wc), BF16)] * CHUNKS
         + [
             pltpu.VMEM((n_date * dates_dev, looks, 128), F32),
             sem((CHUNKS, groups - 1)),

time: 24.3 us -> 23.9 us (0.984)
  Pallas kernels: 22.7 us -> 22.3 us
    pallas_call x1, Pallas kernels: 22.7 us -> 22.3 us  [on_device(): pl.pallas_call(functools.partial(kernel, cfg), out_shape=jax.ShapeDtypeSt...]
where the time goes in v3:
time: 23.9 us; the launch traced here: 23.7 us
  Pallas kernels  22.3 us (93%)
  local copies, waits for them, and re-layouts  0.8 us (3%)
  between operations  0.66 us (3%)
    pallas_call x1, Pallas kernels, on_device(): pl.pallas_call(functools.partial(kernel, cfg), out_shape=jax.ShapeDtypeSt...  22.3 us
    unnamed x1, local copies, waits for them, and re-layouts  0.8 us

profile of v3, /device:TPU:0, one launch (start us, length us, event | category | flops | bytes accessed | tf_op | source)
XLA Modules:
  0.0 23.7 jit_solution(6537703214729365392)
XLA Ops:
  0.7 22.3 %shard_map.46 = f32[66,2,8,128]{3,2,1,0:T(8,128)S(1)} custom-call(bf16[128,1024]{1,0:T(8,128)(2,1)} %bitcast.7, s32[2,128]{1,0:T(2,128)} %bitcast.8, s32[1]{0:T(128)S(6)} %copy.7.valid_ref, s32[2,66]{1,0:T(2,128)} %bitcast.9), custom_call_target="tpu_custom_call" | custom-call | tf_op jit(solution)/shard_map/pallas_call | solution.py:279
  22.9 0.8 %copy.8 = f32[66,1,2,8,128]{4,3,2,1,0:T(8,128)} copy(f32[66,1,2,8,128]{4,3,2,1,0:T(8,128)S(1)} %bitcast.6) | data formatting | bytes 1081344

commit v4 on v3

--- a/solution.py
+++ b/solution.py
@@ -98,7 +98,6 @@
     fetches[0].wait()
     select, place = tables(cfg, foot_ref[...], valid_ref[0], own)
     fetches[1].wait()
-    fetches[2].wait()
 
     def gather_rows(c):
         for part in range(2):
@@ -154,13 +153,6 @@
         tile = jnp.dot(place, rows, preferred_element_type=F32).astype(BF16)
         panels[c][pl.ds(source * dates_dev, dates_dev)] = tile.reshape(dates_dev, blocks, 2 * wc)
 
-    def to_sibling(c, k):
-        for part in range(2):
-            d_copies[c, part, k].wait_recv()
-        fill(c, sources[k])
-        r_copies[c, k] = panel_copy(c, sources[k], f_send.at[c, k], f_recv.at[c, k])
-        r_copies[c, k].start()
-
     def stage_send(c):
         gather_rows(c)
         if c == 0:
@@ -182,7 +174,13 @@
 
     def stage_forward(c):
         for k in range(len(sources)):
-            to_sibling(c, k)
+            for part in range(2):
+                d_copies[c, part, k].wait_recv()
+        for k in range(len(sources)):
+            fill(c, sources[k])
+        for k in range(len(sources)):
+            r_copies[c, k] = panel_copy(c, sources[k], f_send.at[c, k], f_recv.at[c, k])
+            r_copies[c, k].start()
 
     def row_sum(field):
         quads = field.reshape(4, looks, field.shape[1])
@@ -252,6 +250,7 @@
         stage_z(c)
     for c in range(CHUNKS):
         stage_own(c)
+    fetches[2].wait()
     for c in range(CHUNKS):
         stage_forward(c)
         if c > 1:

time: 23.9 us -> 23.5 us (0.983)
  Pallas kernels: 22.3 us -> 21.8 us
    pallas_call x1, Pallas kernels: 22.3 us -> 21.8 us  [on_device(): pl.pallas_call(functools.partial(kernel, cfg), out_shape=jax.ShapeDtypeSt...]
where the time goes in v4:
time: 23.5 us; the launch traced here: 23.3 us
  Pallas kernels  21.8 us (93%)
  local copies, waits for them, and re-layouts  0.8 us (3%)
  between operations  0.66 us (3%)
    pallas_call x1, Pallas kernels, on_device(): pl.pallas_call(functools.partial(kernel, cfg), out_shape=jax.ShapeDtypeSt...  21.8 us
    unnamed x1, local copies, waits for them, and re-layouts  0.8 us

profile of v4, /device:TPU:0, one launch (start us, length us, event | category | flops | bytes accessed | tf_op | source)
XLA Modules:
  0.0 23.3 jit_solution(16401820151867540071)
XLA Ops:
  0.7 21.8 %shard_map.46 = f32[66,2,8,128]{3,2,1,0:T(8,128)S(1)} custom-call(bf16[128,1024]{1,0:T(8,128)(2,1)} %bitcast.7, s32[2,128]{1,0:T(2,128)} %bitcast.8, s32[1]{0:T(128)S(6)} %copy.7.valid_ref, s32[2,66]{1,0:T(2,128)} %bitcast.9), custom_call_target="tpu_custom_call" | custom-call | tf_op jit(solution)/shard_map/pallas_call | solution.py:278
  22.5 0.8 %copy.8 = f32[66,1,2,8,128]{4,3,2,1,0:T(8,128)} copy(f32[66,1,2,8,128]{4,3,2,1,0:T(8,128)S(1)} %bitcast.6) | data formatting | bytes 1081344

commit v5 on v4

--- a/solution.py
+++ b/solution.py
@@ -253,10 +253,9 @@
     fetches[2].wait()
     for c in range(CHUNKS):
         stage_forward(c)
-        if c > 1:
-            stage_looks(c - 2)
-    for c in range(max(CHUNKS - 2, 0), CHUNKS):
-        stage_looks(c)
+        if c > 0:
+            stage_looks(c - 1)
+    stage_looks(CHUNKS - 1)
     for copies in (z_copies, d_copies, s_copies, r_copies):
         for copy in copies.values():
             copy.wait_send()

time: 23.5 us -> 23.2 us (0.987)
    pallas_call x1, Pallas kernels: 21.8 us -> 21.6 us  [on_device(): pl.pallas_call(functools.partial(kernel, cfg), out_shape=jax.ShapeDtypeSt...]
where the time goes in v5:
time: 23.2 us; the launch traced here: 23 us
  Pallas kernels  21.6 us (93%)
  local copies, waits for them, and re-layouts  0.8 us (3%)
  between operations  0.66 us (3%)
    pallas_call x1, Pallas kernels, on_device(): pl.pallas_call(functools.partial(kernel, cfg), out_shape=jax.ShapeDtypeSt...  21.6 us
    unnamed x1, local copies, waits for them, and re-layouts  0.8 us

profile of v5, /device:TPU:0, one launch (start us, length us, event | category | flops | bytes accessed | tf_op | source)
XLA Modules:
  0.0 23.0 jit_solution(14510088907411279147)
XLA Ops:
  0.7 21.6 %shard_map.46 = f32[66,2,8,128]{3,2,1,0:T(8,128)S(1)} custom-call(bf16[128,1024]{1,0:T(8,128)(2,1)} %bitcast.7, s32[2,128]{1,0:T(2,128)} %bitcast.8, s32[1]{0:T(128)S(6)} %copy.7.valid_ref, s32[2,66]{1,0:T(2,128)} %bitcast.9), custom_call_target="tpu_custom_call" | custom-call | tf_op jit(solution)/shard_map/pallas_call | solution.py:277
  22.2 0.8 %copy.8 = f32[66,1,2,8,128]{4,3,2,1,0:T(8,128)} copy(f32[66,1,2,8,128]{4,3,2,1,0:T(8,128)S(1)} %bitcast.6) | data formatting | bytes 1081344

commit v6 on v5

--- a/solution.py
+++ b/solution.py
@@ -8,7 +8,7 @@
 from jax.sharding import PartitionSpec as P
 
 CHUNKS = 4
-BATCH_ROWS, GROUP_ROWS = 1056, 1024
+BATCH_ROWS = 1056
 MESH = pl.DeviceIdType.MESH
 F32, BF16 = jnp.float32, jnp.bfloat16
 
@@ -21,6 +21,11 @@
     chips = n_date // 2
     chip, core = date // 2, date % 2
     sibling = chip * 2 + (1 - core)
+    if chips == 4:
+        x, y = chip % 2, chip // 2
+        near = [y * 2 + 1 - x, (1 - y) * 2 + x, (1 - y) * 2 + 1 - x]
+        others = [near[k] * 2 + core for k in (2, 0, 1)]
+        return sibling, others, others
     targets = [lax.rem(chip + k, chips) * 2 + core for k in range(1, chips)]
     sources = [lax.rem(chip + chips - k, chips) * 2 + core for k in range(1, chips)]
     return sibling, targets, sources
@@ -81,6 +86,7 @@
     dates = n_date * dates_dev
     own, date = lax.axis_index("space"), lax.axis_index("date")
     sibling, targets, sources = partners(date, n_date)
+    across = partners(sibling, n_date)[2]
     peers = [lax.rem(own + k, groups) for k in range(1, groups)]
 
     barrier = pltpu.get_barrier_semaphore()
@@ -192,33 +198,35 @@
         return jnp.dot(rows.astype(BF16), table, preferred_element_type=F32)
 
     def stage_looks(c):
-        s_copies[c].wait_recv()
-        for k in range(len(sources)):
-            r_copies[c, k].wait_recv()
         panel = panels[c]
         col_in = lax.broadcasted_iota(jnp.int32, (wc, 128), 0) + c * wc
         col_out = lax.broadcasted_iota(jnp.int32, (wc, 128), 1)
         table = (jnp.abs(col_in - 4 * col_out - 2) <= 5).astype(F32).astype(BF16)
         last = c == CHUNKS - 1
 
-        group = largest_divisor(dates, max(1, GROUP_ROWS // blocks))
-
-        def power_body(n, carry):
+        def powers(blocks_of):
             sums = []
-            for g in range(group):
-                rows = panel[n * group + g].astype(F32)
-                real, imag = rows[:, :wc], rows[:, wc:]
-                sums.append(row_sum(real * real + imag * imag))
-            looked = col_sum(jnp.concatenate(sums, axis=0), table).reshape(group, looks, 128)
-            at = pl.ds(n * group, group)
-            if c > 0:
-                looked = looked + floor_ref[at]
-            if last:
-                looked = lax.rsqrt(jnp.maximum(looked, 1.0))
-            floor_ref[at] = looked
-            return carry
-
-        lax.fori_loop(0, dates // group, power_body, 0, unroll=True)
+            for source in blocks_of:
+                for d in range(dates_dev):
+                    rows = panel[source * dates_dev + d].astype(F32)
+                    real, imag = rows[:, :wc], rows[:, wc:]
+                    sums.append(row_sum(real * real + imag * imag))
+            looked = col_sum(jnp.concatenate(sums, axis=0), table)
+            looked = looked.reshape(len(blocks_of), dates_dev, looks, 128)
+            for n, source in enumerate(blocks_of):
+                at = pl.ds(source * dates_dev, dates_dev)
+                total = looked[n]
+                if c > 0:
+                    total = total + floor_ref[at]
+                if last:
+                    total = lax.rsqrt(jnp.maximum(total, 1.0))
+                floor_ref[at] = total
+
+        powers([date] + sources)
+        s_copies[c].wait_recv()
+        for k in range(len(sources)):
+            r_copies[c, k].wait_recv()
+        powers([sibling] + across)
 
         batch = largest_divisor(slots, max(1, BATCH_ROWS // blocks))
 

time: 23.2 us -> 23.2 us (level)
  no operation moved by 1% of the time
where the time goes in v6:
time: 23.2 us; the launch traced here: 22.9 us
  Pallas kernels  21.4 us (92%)
  local copies, waits for them, and re-layouts  0.8 us (3%)
  between operations  0.66 us (3%)
    pallas_call x1, Pallas kernels, on_device(): pl.pallas_call(functools.partial(kernel, cfg), out_shape=jax.ShapeDtypeSt...  21.4 us
    unnamed x1, local copies, waits for them, and re-layouts  0.8 us

profile of v6, /device:TPU:0, one launch (start us, length us, event | category | flops | bytes accessed | tf_op | source)
XLA Modules:
  0.0 22.9 jit_solution(1378727876050439116)
XLA Ops:
  0.7 21.4 %shard_map.46 = f32[66,2,8,128]{3,2,1,0:T(8,128)S(1)} custom-call(bf16[128,1024]{1,0:T(8,128)(2,1)} %bitcast.7, s32[2,128]{1,0:T(2,128)} %bitcast.8, s32[1]{0:T(128)S(6)} %copy.7.valid_ref, s32[2,66]{1,0:T(2,128)} %bitcast.9), custom_call_target="tpu_custom_call" | custom-call | tf_op jit(solution)/shard_map/pallas_call | solution.py:285
  22.1 0.8 %copy.8 = f32[66,1,2,8,128]{4,3,2,1,0:T(8,128)} copy(f32[66,1,2,8,128]{4,3,2,1,0:T(8,128)S(1)} %bitcast.6) | data formatting | bytes 1081344

commit v7 on v6

--- a/solution.py
+++ b/solution.py
@@ -256,17 +256,25 @@
         stage_send(c)
     for c in range(CHUNKS):
         stage_z(c)
-    for c in range(CHUNKS):
-        stage_own(c)
+        if c > 0:
+            stage_own(c - 1)
+    stage_own(CHUNKS - 1)
     fetches[2].wait()
     for c in range(CHUNKS):
         stage_forward(c)
         if c > 0:
             stage_looks(c - 1)
+    kinds = (z_copies, d_copies, s_copies, r_copies)
+    early, late = [], []
+    for copies in kinds:
+        for at, copy in copies.items():
+            chunk = at if copies is s_copies else at[0]
+            (late if chunk == CHUNKS - 1 and copies is not z_copies else early).append(copy)
+    for copy in early:
+        copy.wait_send()
     stage_looks(CHUNKS - 1)
-    for copies in (z_copies, d_copies, s_copies, r_copies):
-        for copy in copies.values():
-            copy.wait_send()
+    for copy in late:
+        copy.wait_send()
 
 
 def on_device(slc, footprint, valid_rows, pair_dates):

time: 23.2 us -> 23.1 us (level)
  no operation moved by 1% of the time
where the time goes in v7:
time: 23.1 us; the launch traced here: 22.9 us
  Pallas kernels  21.5 us (93%)
  local copies, waits for them, and re-layouts  0.8 us (3%)
  between operations  0.66 us (3%)
    pallas_call x1, Pallas kernels, on_device(): pl.pallas_call(functools.partial(kernel, cfg), out_shape=jax.ShapeDtypeSt...  21.5 us
    unnamed x1, local copies, waits for them, and re-layouts  0.8 us

profile of v7, /device:TPU:0, one launch (start us, length us, event | category | flops | bytes accessed | tf_op | source)
XLA Modules:
  0.0 22.9 jit_solution(2390272840078582698)
XLA Ops:
  0.7 21.5 %shard_map.46 = f32[66,2,8,128]{3,2,1,0:T(8,128)S(1)} custom-call(bf16[128,1024]{1,0:T(8,128)(2,1)} %bitcast.7, s32[2,128]{1,0:T(2,128)} %bitcast.8, s32[1]{0:T(128)S(6)} %copy.7.valid_ref, s32[2,66]{1,0:T(2,128)} %bitcast.9), custom_call_target="tpu_custom_call" | custom-call | tf_op jit(solution)/shard_map/pallas_call | solution.py:293
  22.1 0.8 %copy.8 = f32[66,1,2,8,128]{4,3,2,1,0:T(8,128)} copy(f32[66,1,2,8,128]{4,3,2,1,0:T(8,128)S(1)} %bitcast.6) | data formatting | bytes 1081344
